TPU v7x, 32 devices: a whole 2x2x4 slice. The times are simulated.
32 devices in a mesh: groups: 2 (over x), point: 8 (over z, y), dp: 2 (over core).
Axes of the slice: x: 2, y: 2, z: 4, core: 2. Of those that a mesh axis runs over, the one named last changes fastest.
Arguments:
- mesh_signals: bfloat16 [4, 32768, 256], P(('groups', 'dp'), 'point'), parts along dimension 0, may hold values from -40 to 40
- payload_linear_map: bfloat16 [256, 256], replicated, may hold values from -0.375 to 0.375
- partition_chooser_map: bfloat16 [256, 256], replicated, may hold values from -0.375 to 0.375
- partition_group_map: bfloat16 [32, 32], replicated, may hold values from -1 to 1
- softness_scale: float32 [8], replicated, may hold values from 0.25 to 1
- centroid_qkv_maps: bfloat16 [3, 32, 32], replicated, may hold values from -1 to 1
- final_linear_map: bfloat16 [256, 256], replicated, may hold values from -0.375 to 0.375
- final_shift_vector: float32 [256], replicated, may hold values from -3 to 3
- upstream_adjoint: bfloat16 [4, 32768, 256], P(('groups', 'dp'), 'point'), parts along dimension 0, may hold values from -6 to 6
Outputs:
- block_response: bfloat16 [4, 32768, 256], P(('groups', 'dp'), 'point'), parts along dimension 0
- input_signal_deriv: bfloat16 [4, 32768, 256], P(('groups', 'dp'), 'point'), parts along dimension 0
- payload_linear_deriv: float32 [512, 256], P('groups'), parts along dimension 0
- partition_chooser_deriv: float32 [512, 256], P('groups'), parts along dimension 0
- partition_group_deriv: float32 [64, 32], P('groups'), parts along dimension 0
- grad_token: float32 [6, 32, 32], P('groups'), parts along dimension 0
- softness_scale_deriv: float32 [16], P('groups'), parts along dimension 0
- final_linear_map_deriv: float32 [512, 256], P('groups'), parts along dimension 0
- shift_vector_deriv: float32 [512], P('groups'), parts along dimension 0
There are 2 independent parts, one for each index of `groups`. A program takes and returns all parts, laid end to end along the dimension named above; an argument that names none is the same for every part. Nothing has to cross between parts.
All inputs are finite; a program needn't handle non-finite values.
Results may differ from a plain program's by a relative error of at most 0.012.
The roundings to bfloat16 on the way count: a program that leaves them out, or rounds other values in their place, can miss the bound.
Values sent between devices are 32-bit elements; how exact they have to be, the bound alone decides.
A program may use at most 128 MiB of HBM per device.

v0:
```python
import math

import jax
import jax.numpy as jnp
from jax import lax
from jax.sharding import PartitionSpec as P

EPS = 1e-05
HIGH = lax.Precision.HIGHEST


def attend(tokens, matrices):
    query = jnp.einsum("shmd,de->shme", tokens, matrices[0], precision=HIGH)
    keys_all = jnp.einsum("shmd,de->shme", tokens, matrices[1], precision=HIGH)
    vals_all = jnp.einsum("shmd,de->shme", tokens, matrices[2], precision=HIGH)
    scores = jnp.einsum("shmd,shnd->shmn", query, keys_all, precision=HIGH) / math.sqrt(
        tokens.shape[-1]
    )
    probs = jax.nn.softmax(scores, axis=-1)
    return jnp.einsum("shmn,shnd->shmd", probs, vals_all, precision=HIGH)


def shards(
    mesh_signals,
    payload_linear_map,
    partition_chooser_map,
    partition_group_map,
    softness_scale,
    centroid_qkv_maps,
    final_linear_map,
    final_shift_vector,
    upstream_adjoint,
):
    f32 = jnp.float32
    bf16 = jnp.bfloat16
    batch_extent, vertex_amount, channel_dimension = mesh_signals.shape
    group_index = softness_scale.shape[0]
    head_size = channel_dimension // group_index
    flat = mesh_signals.reshape(batch_extent * vertex_amount, channel_dimension)
    values = (
        jnp.dot(flat, payload_linear_map, preferred_element_type=f32)
        .astype(bf16)
        .reshape(batch_extent, vertex_amount, group_index, head_size)
    )
    chooser = jnp.dot(flat, partition_chooser_map, preferred_element_type=f32).reshape(
        batch_extent, vertex_amount, group_index, head_size
    )
    head_map = partition_group_map.astype(f32)
    plain_scores = jnp.einsum("sphd,dm->sphm", chooser, head_map, precision=HIGH)
    present_score_entry = plain_scores / softness_scale[:, None]
    weights = jax.nn.softmax(present_score_entry, axis=-1)
    weights_bf = weights.astype(bf16)
    numerator = jnp.einsum("sphm,sphd->shmd", weights_bf, values, preferred_element_type=f32)
    weight_sum = jnp.sum(weights, axis=1)
    numerator, weight_sum = lax.psum((numerator, weight_sum), "point")
    reciprocal = 1.0 / (weight_sum + EPS)
    tokens = numerator * reciprocal[..., None]
    attended, attend_back = jax.vjp(attend, tokens, centroid_qkv_maps.astype(f32))
    attended_bf = attended.astype(bf16)
    mixed = jnp.einsum(
        "sphm,shmd->sphd", weights_bf, attended_bf, preferred_element_type=f32
    ).astype(bf16)
    mixed_flat = mixed.reshape(batch_extent * vertex_amount, channel_dimension)
    block_response = (
        jnp.dot(mixed_flat, final_linear_map, preferred_element_type=f32) + final_shift_vector
    ).astype(bf16)
    grad_flat = upstream_adjoint.reshape(batch_extent * vertex_amount, channel_dimension)
    shift_vector_deriv = jnp.sum(grad_flat.astype(f32), axis=0)
    final_linear_map_deriv = jnp.dot(mixed_flat.T, grad_flat, preferred_element_type=f32)
    scaling_factor = 1.0 / math.sqrt(
        batch_extent * vertex_amount * lax.axis_size("point") * lax.axis_size("dp")
    )
    d_mixed = (
        jnp.dot(grad_flat, final_linear_map.T, preferred_element_type=f32)
        .astype(bf16)
        .reshape(batch_extent, vertex_amount, group_index, head_size)
    )
    d_attended = jnp.einsum("sphm,sphd->shmd", weights_bf, d_mixed, preferred_element_type=f32)
    d_attended = lax.psum(d_attended, "point")
    d_tokens, centroid_qkv_deriv = attend_back(d_attended)
    d_numerator = (d_tokens * reciprocal[..., None]).astype(bf16)
    d_weight_sum = -jnp.sum(d_tokens * tokens, axis=-1) * reciprocal
    d_weights = jnp.einsum("sphd,shmd->sphm", d_mixed, attended_bf, preferred_element_type=f32)
    d_weights = d_weights + jnp.einsum(
        "sphd,shmd->sphm", values, d_numerator, preferred_element_type=f32
    )
    d_weights = d_weights + d_weight_sum[:, None]
    score_deriv = weights * (d_weights - jnp.sum(weights * d_weights, axis=-1, keepdims=True))
    direct_adjoint = score_deriv / softness_scale[:, None]
    softness_scale_deriv = (
        -jnp.sum(score_deriv * present_score_entry, axis=(0, 1, 3)) / softness_scale
    )
    partition_group_deriv = jnp.einsum("sphd,sphm->dm", chooser, direct_adjoint, precision=HIGH)
    d_chooser = (
        jnp.einsum("sphm,dm->sphd", direct_adjoint, head_map, precision=HIGH)
        .astype(bf16)
        .reshape(batch_extent * vertex_amount, channel_dimension)
    )
    d_values = (
        jnp.einsum("sphm,shmd->sphd", weights_bf, d_numerator, preferred_element_type=f32)
        .astype(bf16)
        .reshape(batch_extent * vertex_amount, channel_dimension)
    )
    input_signal_deriv = (
        jnp.dot(d_values, payload_linear_map.T, preferred_element_type=f32)
        + jnp.dot(d_chooser, partition_chooser_map.T, preferred_element_type=f32)
    ).astype(bf16)
    payload_linear_deriv = jnp.dot(flat.T, d_values, preferred_element_type=f32)
    partition_chooser_deriv = jnp.dot(flat.T, d_chooser, preferred_element_type=f32)
    (
        payload_linear_deriv,
        partition_chooser_deriv,
        partition_group_deriv,
        softness_scale_deriv,
        final_linear_map_deriv,
        shift_vector_deriv,
    ) = lax.psum(
        (
            payload_linear_deriv,
            partition_chooser_deriv,
            partition_group_deriv,
            softness_scale_deriv,
            final_linear_map_deriv,
            shift_vector_deriv,
        ),
        ("point", "dp"),
    )
    centroid_qkv_deriv = lax.psum(centroid_qkv_deriv, "dp")
    return (
        block_response.reshape(batch_extent, vertex_amount, channel_dimension),
        input_signal_deriv.reshape(batch_extent, vertex_amount, channel_dimension),
        payload_linear_deriv * scaling_factor,
        partition_chooser_deriv * scaling_factor,
        partition_group_deriv * scaling_factor,
        centroid_qkv_deriv * scaling_factor,
        softness_scale_deriv * scaling_factor,
        final_linear_map_deriv * scaling_factor,
        shift_vector_deriv * scaling_factor,
    )


def solution(mesh):
    placed = (
        P(("groups", "dp"), "point", None),
        P(),
        P(),
        P(),
        P(),
        P(),
        P(),
        P(),
        P(("groups", "dp"), "point", None),
    )
    return jax.shard_map(
        shards,
        mesh=mesh,
        in_specs=placed,
        out_specs=(
            P(("groups", "dp"), "point", None),
            P(("groups", "dp"), "point", None),
            P("groups", None),
            P("groups", None),
            P("groups", None),
            P("groups", None, None),
            P("groups"),
            P("groups", None),
            P("groups"),
        ),
        check_vma=False,
    )
```

profile of v0, /device:TPU:29, one launch (start us, length us, event | category | flops | bytes accessed | tf_op | source)
XLA Modules:
  0.0 306.7 jit_solution(16892384534982088988)
XLA Ops:
  9.6 1.9 copy-done.23
  11.5 2.6 convolution_divide_fusion
  14.2 8.9 %fusion.81 = (f32[4096,8]{0,1:T(8,128)S(1)}, f32[4096,8,32]{0,2,1:T(8,128)S(1)}) fusion(f32[4096,8,32]{0,2,1:T(8,128)S(1)} %convolution_divide_fusion), kind=kOutput, calls=%fused_computation.114 | output fusion | flops 2097183 | bytes 8519680 | tf_op jit(solution)/shard_map/sub | solution.py:51
  23.9 1.3 fusion.79
  25.2 1.3 convolution_bitcast_fusion.1
  27.8 1.4 fusion.83
  29.3 2.1 convert_reduce_fusion
  31.4 66.9 %all-reduce.11.cloned.1.call-done = (f32[1,8,32,32]{3,2,1,0:T(8,128)}, f32[1,8,32]{2,1,0:T(8,128)}, f32[8,32,32]{2,1,0:T(8,128)}) async-done(((f32[1,8,32,32]{3,2,1,0:T(8,128)}, f32[1,8,32]{2,1,0:T(8,128)}, f32[8,32,32]{2,1,0:T(8,128)}), (f32[1,8,32,32]{3,2,1,0:T(8,128)}, f32[1,8,32]{2,1,0:T(8,128)}, f32[8,32,32]{2,1,0:T(8,128)})) %all-reduce.11.cloned.1.call-update) | async-done | bytes 66576 | tf_op jit(solution)/shard_map/psum | solution.py:55
  103.1 1.3 convolution_bitcast_fusion
  104.4 1.3 multiply_reduce_fusion
  106.4 1.4 convolution_bitcast_fusion.4
  111.0 1.9 fusion.14
  115.3 4.4 %fusion.31 = f32[32,32]{1,0:T(8,128)S(1)} fusion(f32[4096,8,32]{0,2,1:T(8,128)S(1)} %copy-done.24, f32[8]{0:T(128)S(1)} %copy-done.22, f32[1,4096,8,32]{1,3,2,0:T(8,128)S(1)} %get-tuple-element.47, f32[4096,8]{0,1:T(8,128)S(1)} %get-tuple-element.46, f32[4096,8,32]{0,2,1:T(8,128)S(1)} %copy-done.4, f32[4096,8]{0,1:T(8,128)S(1)} %get-tuple-element.38), kind=kOutput, calls=%fused_computation.48 | convolution fusion | flops 406847488 | bytes 12849184 | tf_op jit(solution)/shard_map/sphd,sphm->dm/dot_general | solution.py:93
  119.7 4.4 %convolution_convert_fusion = bf16[4096,8,32]{0,2,1:T(8,128)(2,1)} fusion(bf16[32,32]{1,0:T(8,128)(2,1)S(1)} %copy-done.20, f32[8]{0:T(128)S(1)} %copy-done.22, f32[1,4096,8,32]{1,3,2,0:T(8,128)S(1)} %get-tuple-element.47, f32[4096,8]{0,1:T(8,128)S(1)} %get-tuple-element.46, f32[4096,8,32]{0,2,1:T(8,128)S(1)} %copy-done.4, f32[4096,8]{0,1:T(8,128)S(1)} %get-tuple-element.38), kind=kOutput, calls=%fused_computation.11 | convolution fusion | flops 407896064 | bytes 10749984 | tf_op jit(solution)/shard_map/sphm,dm->sphd/dot_general | solution.py:95
  124.9 2.1 convolution_convert_fusion.3
  127.0 1.4 fusion.28
  128.4 2.7 fusion.84
  131.1 5.6 %psum.76 = f32[3,32,32]{2,1,0:T(8,128)S(1)} all-reduce(f32[3,32,32]{2,1,0:T(8,128)S(1)} %pad_add_fusion), channel_id=1, replica_groups=mesh['groups'=2,'point'=8,'dp'=2] {'dp'}, use_global_device_ids=true, to_apply=%region_14.0 | all-reduce | flops 3072 | bytes 24576 | tf_op jit(solution)/shard_map/psum | solution.py:128
  137.3 57.0 %all-reduce.3 = (f32[32,32]{1,0:T(8,128)S(1)}, f32[8]{0:T(128)S(1)}, f32[256]{0:T(256)S(1)}) all-reduce(f32[32,32]{1,0:T(8,128)S(1)} %fusion.31, f32[8]{0:T(128)S(1)} %negate_divide_fusion, f32[256]{0:T(256)S(1)} %convert_reduce_fusion), channel_id=1, replica_groups=mesh['groups'=2,'point'=8,'dp'=2] {'point','dp'}, use_global_device_ids=true, to_apply=%region_13.0 | all-reduce | flops 1288 | bytes 10304 | tf_op jit(solution)/shard_map/psum | solution.py:117
  195.5 3.1 %fusion.25 = f32[256,256]{0,1:T(8,128)} fusion(bf16[4096,256]{0,1:T(8,128)(2,1)} %bitcast.196, bf16[1,4096,256]{2,1,0:T(8,128)(2,1)S(1)} %copy-done), kind=kOutput, calls=%fused_computation.40 | convolution fusion | flops 536870912 | bytes 4456448 | tf_op jit(solution)/shard_map/dot_general | solution.py:109
  198.6 1.7 fusion.15
  200.3 3.7 %fusion.9 = bf16[1,4096,256]{2,1,0:T(8,128)(2,1)} fusion(bf16[4096,256]{0,1:T(8,128)(2,1)} %bitcast.194, bf16[256,256]{1,0:T(8,128)(2,1)S(1)} %copy-done.17, f32[256]{0:T(256)S(1)} %copy-done.21), kind=kOutput, calls=%fused_computation.17 | convolution fusion | flops 538968064 | bytes 4326400 | tf_op jit(solution)/shard_map/dot_general | solution.py:65
  204.5 4.9 %fusion.8 = bf16[1,4096,256]{2,1,0:T(8,128)(2,1)} fusion(f32[4096,256]{1,0:T(8,128)} %fusion.84, bf16[4096,256]{0,1:T(8,128)(2,1)} %bitcast.197, bf16[256,256]{1,0:T(8,128)(2,1)S(1)} %copy-done.16), kind=kOutput, calls=%fused_computation.16 | convolution fusion | flops 538968064 | bytes 8519680 | tf_op jit(solution)/shard_map/dot_general | solution.py:106
  209.4 85.9 %all-reduce.9.cloned.1.call-done = (f32[256,256]{0,1:T(8,128)}, f32[256,256]{0,1:T(8,128)}, f32[256,256]{0,1:T(8,128)}) async-done(((f32[256,256]{0,1:T(8,128)}, f32[256,256]{0,1:T(8,128)}, f32[256,256]{0,1:T(8,128)}), (f32[256,256]{0,1:T(8,128)}, f32[256,256]{0,1:T(8,128)}, f32[256,256]{0,1:T(8,128)})) %all-reduce.9.cloned.1.call-update) | async-done | bytes 786448 | tf_op jit(solution)/shard_map/psum | solution.py:117
  (88 shorter events, 23.1 us)
Async XLA Ops:
  7.2 4.3 %copy-start.20 = (bf16[32,32]{1,0:T(8,128)(2,1)S(1)}, bf16[32,32]{1,0:T(8,128)(2,1)}, u32[]{:S(2)}) copy-start(bf16[32,32]{1,0:T(8,128)(2,1)} %param.12) | copy-start | bytes 6148
  7.2 4.3 %copy-start.22 = (f32[8]{0:T(128)S(1)}, f32[8]{0:T(128)}, u32[]{:S(2)}) copy-start(f32[8]{0:T(128)} %param.13) | copy-start | bytes 100
  7.2 91.1 %all-reduce.11.cloned.1.call-start = ((), (), s32[]{:S(2)}) async-start(), calls=%async_computation.1 | async-start | bytes 532480 | tf_op jit(solution)/shard_map/psum | solution.py:55
  14.2 8.9 %copy-start.9 = (f32[4096,8,32]{0,2,1:T(8,128)}, f32[4096,8,32]{0,2,1:T(8,128)S(1)}, u32[]{:S(2)}) copy-start(f32[4096,8,32]{0,2,1:T(8,128)S(1)} %convolution_divide_fusion) | copy-start | bytes 12582916
  14.2 8.9 %copy-start.15 = (bf16[256,256]{1,0:T(8,128)(2,1)S(1)}, bf16[256,256]{1,0:T(8,128)(2,1)}, u32[]{:S(2)}) copy-start(bf16[256,256]{1,0:T(8,128)(2,1)} %param.10) | copy-start | bytes 393220
  23.1 2.1 copy-start.3
  23.9 2.7 copy-start.11
  23.9 3.1 %copy-start.7 = (bf16[1,4096,256]{2,1,0:T(8,128)(2,1)S(1)}, bf16[1,4096,256]{2,1,0:T(8,128)(2,1)}, u32[]{:S(2)}) copy-start(bf16[1,4096,256]{2,1,0:T(8,128)(2,1)} %param.17) | copy-start | bytes 6291460
  23.9 3.1 %copy-start.17 = (bf16[256,256]{1,0:T(8,128)(2,1)S(1)}, bf16[256,256]{1,0:T(8,128)(2,1)}, u32[]{:S(2)}) copy-start(bf16[256,256]{1,0:T(8,128)(2,1)} %param.15) | copy-start | bytes 393220
  25.2 2.6 copy-start.1
  27.8 71.4 %copy-start.18 = (bf16[3,32,32]{2,1,0:T(8,128)(2,1)S(1)}, bf16[3,32,32]{2,1,0:T(8,128)(2,1)}, u32[]{:S(2)}) copy-start(bf16[3,32,32]{2,1,0:T(8,128)(2,1)} %param.14) | copy-start | bytes 18436
  29.2 266.1 %all-reduce.9.cloned.1.call-start = ((), (), s32[]{:S(2)}) async-start(), calls=%async_computation | async-start | bytes 1572864 | tf_op jit(solution)/shard_map/psum | solution.py:117
  98.3 10.2 %copy-start.14 = (f32[1,8,32,32]{3,2,1,0:T(8,128)S(1)}, f32[1,8,32,32]{3,2,1,0:T(8,128)}, u32[]{:S(2)}) copy-start(f32[1,8,32,32]{3,2,1,0:T(8,128)} %get-tuple-element.33) | copy-start | bytes 98308
  98.3 11.6 %copy-start.19 = (f32[1,8,32]{2,1,0:T(8,128)S(1)}, f32[1,8,32]{2,1,0:T(8,128)}, u32[]{:S(2)}) copy-start(f32[1,8,32]{2,1,0:T(8,128)} %get-tuple-element.34) | copy-start | bytes 3076
  98.3 11.6 %copy-start.6 = (bf16[4096,256]{0,1:T(8,128)(2,1)S(1)}, bf16[4096,256]{0,1:T(8,128)(2,1)}, u32[]{:S(2)}) copy-start(bf16[4096,256]{0,1:T(8,128)(2,1)} %copy-done.5) | copy-start | bytes 6291460
  108.1 2.6 copy-start.4
  108.1 2.9 copy-start.12
  111.0 2.2 copy-start.10
  113.1 2.2 copy-start.24
  119.7 4.4 %copy-start.2 = (bf16[4096,8,32]{0,2,1:T(8,128)(2,1)S(1)}, bf16[4096,8,32]{0,2,1:T(8,128)(2,1)}, u32[]{:S(2)}) copy-start(bf16[4096,8,32]{0,2,1:T(8,128)(2,1)} %copy-done.1) | copy-start | bytes 6291460
  194.3 4.3 %copy-start.8 = (bf16[1,4096,256]{2,1,0:T(8,128)(2,1)S(1)}, bf16[1,4096,256]{2,1,0:T(8,128)(2,1)}, u32[]{:S(2)}) copy-start(bf16[1,4096,256]{2,1,0:T(8,128)(2,1)} %param.17) | copy-start | bytes 6291460
  194.3 4.3 %copy-start.13 = (bf16[8,32,4096]{2,1,0:T(8,128)(2,1)S(1)}, bf16[8,32,4096]{2,1,0:T(8,128)(2,1)}, u32[]{:S(2)}) copy-start(bf16[8,32,4096]{2,1,0:T(8,128)(2,1)} %convolution_convert_fusion.3) | copy-start | bytes 6291460
  195.5 4.8 %copy-start.21 = (f32[256]{0:T(256)S(1)}, f32[256]{0:T(256)}, u32[]{:S(2)}) copy-start(f32[256]{0:T(256)} %param.16) | copy-start | bytes 3076
  200.3 4.2 %copy-start.16 = (bf16[256,256]{1,0:T(8,128)(2,1)S(1)}, bf16[256,256]{1,0:T(8,128)(2,1)}, u32[]{:S(2)}) copy-start(bf16[256,256]{1,0:T(8,128)(2,1)} %param.11) | copy-start | bytes 393220
  (3 other events, 5.0 us)
Sparse Core Ops, SparseCore 0:
  29.4 68.9 all-reduce.10
  204.1 91.1 all-reduce.8
where the time goes:
time: 312 us; the launch traced here: 307 us
  waiting for transfers between devices  153 us (49%)
  blocking collectives  62.5 us (20%)
  matrix products  49.9 us (16%)
  other arithmetic  18.6 us (6%)
  between operations  14.5 us (5%)
  local copies, waits for them, and re-layouts  8.31 us (3%)
    psum x1, waiting for transfers between devices, shards(): lax.psum((payload_linear_deriv, partition_chooser_deriv, partition_group_...  85.9 us
    psum x1, waiting for transfers between devices, shards(): numerator, weight_sum = lax.psum((numerator, weight_sum), 'point')  66.9 us
    psum x1, blocking collectives, shards(): lax.psum((payload_linear_deriv, partition_chooser_deriv, partition_group_...  57 us
    sub x1, other arithmetic, shards(): weights = jax.nn.softmax(present_score_entry, axis=-1)  8.92 us
    unnamed x54, local copies, waits for them, and re-layouts  8.31 us
  transfers between devices with their start and end apart: 2, of which 2 were waited for; matrix products, arithmetic and copies ran while one was open for 2% of the time, Pallas kernels for 0%

commit v1 on v0

v1 whole, which is shorter than its diff:
```python
import functools
import math

import jax
import jax.numpy as jnp
from jax import lax
from jax.experimental import pallas as pl
from jax.experimental.pallas import tpu as pltpu
from jax.sharding import PartitionSpec as P

EPS = 1e-05
HIGH = lax.Precision.HIGHEST
F32 = jnp.float32
BF16 = jnp.bfloat16
VMEM_LIMIT = 56 * 1024 * 1024


def nt(a, b, precision=None):
    return lax.dot_general(
        a, b, (((1,), (1,)), ((), ())), precision=precision, preferred_element_type=F32
    )


def nn(a, b, precision=None):
    return lax.dot_general(
        a, b, (((1,), (0,)), ((), ())), precision=precision, preferred_element_type=F32
    )


def tn(a, b, precision=None):
    return lax.dot_general(
        a, b, (((0,), (0,)), ((), ())), precision=precision, preferred_element_type=F32
    )


def block_mask(size, head):
    row = lax.broadcasted_iota(jnp.int32, (size, size), 0) // head
    col = lax.broadcasted_iota(jnp.int32, (size, size), 1) // head
    return row == col


def fold(square, mask, heads, head):
    kept = jnp.where(mask, square, 0.0)
    return jnp.sum(kept.reshape(heads, head, heads * head), axis=0)


def unfold(flat, mask, heads):
    return jnp.where(mask, jnp.concatenate([flat] * heads, axis=0), 0.0)


def forward_kernel(
    heads, x_ref, u_ref, wp_ref, hi_ref, lo_ref, wf_ref, vt_ref, wt_ref, dmt_ref, sums_ref, acc, wacc
):
    step = pl.program_id(0)
    size, rows = wt_ref.shape
    head = size // heads
    x = x_ref[...]
    values = nt(wp_ref[...], x).astype(BF16)
    logit = nt(hi_ref[...], x) + nt(lo_ref[...], x)
    d_mixed = nt(wf_ref[...], u_ref[...]).astype(BF16)
    logit = logit.reshape(heads, head, rows)
    top = jnp.max(logit, axis=1, keepdims=True)
    grown = jnp.exp(logit - top)
    share = 1.0 / jnp.sum(grown, axis=1, keepdims=True)
    weights = (grown * share).reshape(size, rows)
    weights_bf = weights.astype(BF16)
    vt_ref[...] = values
    dmt_ref[...] = d_mixed
    wt_ref[...] = weights
    both = nt(weights_bf, jnp.concatenate([values, d_mixed], axis=0))
    lanes = wacc.shape[1]
    part = weights[:, :lanes]
    for i in range(1, rows // lanes):
        part = part + weights[:, i * lanes : (i + 1) * lanes]

    @pl.when(step == 0)
    def _():
        acc[...] = both
        wacc[...] = part

    @pl.when(step > 0)
    def _():
        acc[...] += both
        wacc[...] += part

    @pl.when(step == pl.num_programs(0) - 1)
    def _():
        mask = block_mask(size, head)
        total = jnp.sum(wacc[...], axis=1, keepdims=True)
        sums_ref[0:head, :] = fold(acc[:, :size], mask, heads, head)
        sums_ref[head : 2 * head, :] = fold(acc[:, size:], mask, heads, head)
        sums_ref[2 * head : 3 * head, :] = fold(
            jnp.broadcast_to(total, (size, size)), mask, heads, head
        )
        spare = sums_ref.shape[0] - 3 * head
        if spare:
            sums_ref[3 * head :, :] = jnp.zeros((spare, size), F32)


def token_kernel(heads, sums_ref, maps_ref, att_ref, dnum_ref, dws_ref, dmap_ref):
    size = maps_ref.shape[1]
    head = size // heads
    mask = block_mask(size, head)
    numerator = unfold(sums_ref[0:head, :], mask, heads)
    d_att = unfold(sums_ref[head : 2 * head, :], mask, heads)
    spread = unfold(sums_ref[2 * head : 3 * head, :], mask, heads)
    weight_sum = jnp.sum(spread, axis=1, keepdims=True) * (1.0 / head)
    reciprocal = 1.0 / (weight_sum + EPS)
    tokens = numerator * reciprocal
    maps = [maps_ref[i] for i in range(3)]
    q, k, v = (nn(tokens, w, HIGH) for w in maps)
    root = 1.0 / math.sqrt(head)
    scores = jnp.where(mask, nt(q, k, HIGH) * root, -jnp.inf)
    grown = jnp.exp(scores - jnp.max(scores, axis=1, keepdims=True))
    probs = grown / jnp.sum(grown, axis=1, keepdims=True)
    attended = nn(probs, v, HIGH)
    d_v = tn(probs, d_att, HIGH)
    d_probs = nt(d_att, v, HIGH)
    d_scores = probs * (d_probs - jnp.sum(probs * d_probs, axis=1, keepdims=True)) * root
    d_q = nn(d_scores, k, HIGH)
    d_k = tn(d_scores, q, HIGH)
    d_tokens = nt(d_q, maps[0], HIGH) + nt(d_k, maps[1], HIGH) + nt(d_v, maps[2], HIGH)
    att_ref[...] = attended.astype(BF16)
    dnum_ref[...] = (d_tokens * reciprocal).astype(BF16)
    dws = -jnp.sum(d_tokens * tokens, axis=1, keepdims=True) * reciprocal
    dws_ref[...] = jnp.broadcast_to(dws, dws_ref.shape)
    for i, d in enumerate((d_q, d_k, d_v)):
        dmap_ref[i] = fold(tn(tokens, d, HIGH), mask, heads, head)


def backward_kernel(
    heads, points,
    x_ref, u_ref, vt_ref, wt_ref, dmt_ref, att_ref, dnum_ref, dws_ref,
    wp_ref, hi_ref, lo_ref, wf_ref, shift_ref, dmap_ref,
    resp_ref, din_ref, grads_ref,
):
    step = pl.program_id(0)
    size, rows = wt_ref.shape
    head = size // heads
    u = u_ref[...]
    x = x_ref[...]
    weights = wt_ref[...]
    weights_bf = weights.astype(BF16)
    mixed = tn(att_ref[...], weights_bf).astype(BF16)
    d_values = tn(dnum_ref[...], weights_bf).astype(BF16)
    resp_ref[...] = (tn(mixed, wf_ref[...]) + shift_ref[...]).astype(BF16)
    d_weights = nn(att_ref[...], dmt_ref[...]) + nn(dnum_ref[...], vt_ref[...])
    d_weights = d_weights + dws_ref[:, 0:1]
    product = (weights * d_weights).reshape(heads, head, rows)
    mean = jnp.sum(product, axis=1, keepdims=True)
    d_logit = (product - weights.reshape(heads, head, rows) * mean).reshape(size, rows)
    d_high = d_logit.astype(BF16)
    d_low = (d_logit - d_high.astype(F32)).astype(BF16)
    din_ref[...] = (
        tn(d_values, wp_ref[...])
        + tn(d_high, hi_ref[...])
        + tn(d_high, lo_ref[...])
        + tn(d_low, hi_ref[...])
    ).astype(BF16)
    ones = jnp.ones((8, rows), BF16)
    parts = (nn(d_values, x), nn(d_high, x) + nn(d_low, x), nn(mixed, u), nn(ones, u))
    spans = ((0, size), (size, 2 * size), (2 * size, 3 * size), (3 * size, 3 * size + 8))

    @pl.when(step == 0)
    def _():
        for (a, b), part in zip(spans, parts):
            grads_ref[a:b, :] = part
        tail = 3 * size + 8
        end = tail + 3 * head
        grads_ref[tail:end, :] = dmap_ref[...] * (1.0 / points)
        spare = grads_ref.shape[0] - end
        if spare:
            grads_ref[end:, :] = jnp.zeros((spare, size), F32)

    @pl.when(step > 0)
    def _():
        for (a, b), part in zip(spans, parts):
            grads_ref[a:b, :] += part


def reduce_kernel(n, paired, x_ref, out_ref, recv, full, rs_sem, ag_sem, *more):
    me = lax.axis_index("point")
    core = lax.axis_index("dp")
    peers = [lax.rem(me + o, n) for o in range(1, n)]
    mesh_id = pl.DeviceIdType.MESH
    barrier = pltpu.get_barrier_semaphore()
    for peer in peers:
        pl.semaphore_signal(barrier, inc=1, device_id={"point": peer}, device_id_type=mesh_id)
    if paired:
        pl.semaphore_signal(barrier, inc=1, device_id={"dp": 1 - core}, device_id_type=mesh_id)
    pl.semaphore_wait(barrier, n if paired else n - 1)

    def send(src, dst, sems, slot, target):
        copy = pltpu.make_async_remote_copy(
            src_ref=src, dst_ref=dst, send_sem=sems.at[0, slot], recv_sem=sems.at[1, slot],
            device_id=target, device_id_type=mesh_id,
        )
        copy.start()
        return copy

    if paired:
        swapped, half, swap_sem, pass_sem = more
        swaps = [
            send(x_ref.at[1 - core, k], swapped.at[k], swap_sem, k, {"dp": 1 - core})
            for k in range(n)
        ]
        for k in range(n):
            swaps[k].wait_recv()
            half[k] = x_ref[core, k] + swapped[k]
        source, target = half, full.at[core]
    else:
        source, target = x_ref, full
    scatter = [
        send(source.at[peer], recv.at[o], rs_sem, o, {"point": peer})
        for o, peer in enumerate(peers)
    ]
    total = source[me]
    for o, copy in enumerate(scatter):
        copy.wait_recv()
        total = total + recv[o]
    target[me] = total
    gather = [
        send(target.at[me], target.at[me], ag_sem, o, {"point": peer})
        for o, peer in enumerate(peers)
    ]
    passed = []
    if paired:
        passed.append(send(target.at[me], target.at[me], pass_sem, 0, {"dp": 1 - core}))
    for o, copy in enumerate(gather):
        copy.wait_recv()
        if paired:
            owner = lax.rem(me + n - (o + 1), n)
            passed.append(
                send(target.at[owner], target.at[owner], pass_sem, o + 1, {"dp": 1 - core})
            )
    if paired:
        for copy in passed:
            copy.wait_recv()
        for copy in swaps + passed:
            copy.wait_send()
    for copy in scatter + gather:
        copy.wait_send()
    out_ref[...] = full[...]


def reduce_over(x, n, paired):
    rows, size = x.shape
    r = rows // (2 * n if paired else n)
    shape = (2, n, r, size) if paired else (n, r, size)
    dma = pltpu.SemaphoreType.DMA
    scratch = [
        pltpu.VMEM((n - 1, r, size), F32), pltpu.VMEM(shape, F32), dma((2, n - 1)), dma((2, n - 1)),
    ]
    if paired:
        scratch += [
            pltpu.VMEM((n, r, size), F32), pltpu.VMEM((n, r, size), F32), dma((2, n)), dma((2, n)),
        ]
    out = pl.pallas_call(
        functools.partial(reduce_kernel, n, paired),
        out_shape=jax.ShapeDtypeStruct(shape, F32),
        in_specs=[pl.BlockSpec(memory_space=pltpu.VMEM)],
        out_specs=pl.BlockSpec(memory_space=pltpu.VMEM),
        scratch_shapes=scratch,
        compiler_params=pltpu.CompilerParams(
            collective_id=1 if paired else 0, has_side_effects=True, vmem_limit_bytes=VMEM_LIMIT
        ),
    )(x.reshape(shape))
    return out.reshape(rows, size)


def padded(rows, pieces):
    return pieces * 8 * -(-rows // (pieces * 8))


def spread_heads(small, heads):
    return jnp.kron(jnp.eye(heads, dtype=small.dtype), small)


def shards(
    mesh_signals,
    payload_linear_map,
    partition_chooser_map,
    partition_group_map,
    softness_scale,
    centroid_qkv_maps,
    final_linear_map,
    final_shift_vector,
    upstream_adjoint,
):
    batch, points, size = mesh_signals.shape
    heads = softness_scale.shape[0]
    head = size // heads
    x = mesh_signals.reshape(points, size)
    u = upstream_adjoint.reshape(points, size)
    rows = 512
    steps = points // rows
    n_point = lax.axis_size("point")
    sum_rows = padded(3 * head, n_point)
    grad_rows = padded(3 * size + 8 + 3 * head, 2 * n_point)
    inverse = jnp.repeat(1.0 / softness_scale, head)
    group_square = spread_heads(partition_group_map.astype(F32), heads)
    joined = jnp.dot(partition_chooser_map.astype(F32), group_square, precision=HIGH) * inverse
    joined_t = joined.T
    rounded = lax.reduce_precision(joined_t, 8, 7)
    hi = rounded.astype(BF16)
    lo = (joined_t - rounded).astype(BF16)
    params = pltpu.CompilerParams(
        dimension_semantics=("arbitrary",), vmem_limit_bytes=VMEM_LIMIT
    )
    tall = pl.BlockSpec((rows, size), lambda i: (i, 0))
    wide = pl.BlockSpec((size, rows), lambda i: (0, i))

    def whole(*shape):
        return pl.BlockSpec(shape, lambda i: (0,) * len(shape))

    square = whole(size, size)
    vt, wt, dmt, sums = pl.pallas_call(
        functools.partial(forward_kernel, heads),
        grid=(steps,),
        in_specs=[tall, tall, square, square, square, square],
        out_specs=[wide, wide, wide, whole(sum_rows, size)],
        out_shape=[
            jax.ShapeDtypeStruct((size, points), BF16),
            jax.ShapeDtypeStruct((size, points), F32),
            jax.ShapeDtypeStruct((size, points), BF16),
            jax.ShapeDtypeStruct((sum_rows, size), F32),
        ],
        scratch_shapes=[pltpu.VMEM((size, 2 * size), F32), pltpu.VMEM((size, 128), F32)],
        compiler_params=params,
    )(x, u, payload_linear_map.T, hi, lo, final_linear_map)
    sums = reduce_over(sums, n_point, False)
    maps = jnp.stack([spread_heads(centroid_qkv_maps[i].astype(F32), heads) for i in range(3)])
    att, dnum, dws, dmap = pl.pallas_call(
        functools.partial(token_kernel, heads),
        out_shape=[
            jax.ShapeDtypeStruct((size, size), BF16),
            jax.ShapeDtypeStruct((size, size), BF16),
            jax.ShapeDtypeStruct((size, 128), F32),
            jax.ShapeDtypeStruct((3, head, size), F32),
        ],
        compiler_params=pltpu.CompilerParams(vmem_limit_bytes=VMEM_LIMIT),
    )(sums, maps)
    resp, din, grads = pl.pallas_call(
        functools.partial(backward_kernel, heads, n_point),
        grid=(steps,),
        in_specs=[
            tall, tall, wide, wide, wide, square, square, whole(size, 128),
            square, square, square, square, whole(1, size), whole(3 * head, size),
        ],
        out_specs=[tall, tall, whole(grad_rows, size)],
        out_shape=[
            jax.ShapeDtypeStruct((points, size), BF16),
            jax.ShapeDtypeStruct((points, size), BF16),
            jax.ShapeDtypeStruct((grad_rows, size), F32),
        ],
        compiler_params=params,
    )(
        x, u, vt, wt, dmt, att, dnum, dws,
        payload_linear_map.T, hi, lo, final_linear_map, final_shift_vector[None, :],
        dmap.reshape(3 * head, size),
    )
    grads = reduce_over(grads, n_point, True)
    tail = 3 * size + 8
    d_maps = jnp.sum(grads[tail : tail + 3 * head].reshape(3, head, heads, head), axis=2)
    scaling = 1.0 / math.sqrt(
        batch * points * lax.axis_size("point") * lax.axis_size("dp")
    )
    payload_deriv = grads[:size].T * scaling
    logit_deriv = grads[size : 2 * size].T
    raw_deriv = logit_deriv * (inverse * scaling)
    chooser_deriv = jnp.dot(raw_deriv, group_square.T, precision=HIGH)
    crossed = jnp.dot(partition_chooser_map.astype(F32).T, raw_deriv, precision=HIGH)
    crossed = crossed.reshape(heads, head, heads, head)
    group_deriv = sum(crossed[h, :, h] for h in range(heads))
    softness_deriv = -scaling * jnp.sum((joined * logit_deriv).reshape(size, heads, head), axis=(0, 2))
    softness_deriv = softness_deriv / softness_scale
    return (
        resp.reshape(batch, points, size),
        din.reshape(batch, points, size),
        payload_deriv,
        chooser_deriv,
        group_deriv,
        d_maps * scaling,
        softness_deriv,
        grads[2 * size : 3 * size] * scaling,
        grads[3 * size] * scaling,
    )


def solution(mesh):
    placed = (
        P(("groups", "dp"), "point", None),
        P(),
        P(),
        P(),
        P(),
        P(),
        P(),
        P(),
        P(("groups", "dp"), "point", None),
    )
    return jax.shard_map(
        shards,
        mesh=mesh,
        in_specs=placed,
        out_specs=(
            P(("groups", "dp"), "point", None),
            P(("groups", "dp"), "point", None),
            P("groups", None),
            P("groups", None),
            P("groups", None),
            P("groups", None, None),
            P("groups"),
            P("groups", None),
            P("groups"),
        ),
        check_vma=False,
    )
```

time: 312 us -> 101 us (0.32); the launches traced: 307 us -> 99.6 us
  waiting for transfers between devices: 153 us -> 0 us
  Pallas kernels: 0 us -> 77.2 us
  blocking collectives: 62.5 us -> 0 us
  matrix products: 49.9 us -> 4.75 us
  between operations: 14.5 us -> 0.78 us
  other arithmetic: 18.6 us -> 8.64 us
    psum x2 -> x0, waiting for transfers between devices: 153 us -> none  [the longest x1 85.9 us: shards(): lax.psum((payload_linear_deriv, partition_chooser_deriv, partition_group_...]
    pallas_call x0 -> x5, Pallas kernels: none -> 77.2 us  [the longest x2 43.2 us: reduce_over(): pl.pallas_call(functools.partial(reduce_kernel, n, paired), out_shape=jax...]
    psum x2 -> x0, blocking collectives: 62.5 us -> none  [the longest x1 57 us: shards(): lax.psum((payload_linear_deriv, partition_chooser_deriv, partition_group_...]
    dot_general x33 -> x3, matrix products: 49.9 us -> 4.75 us  [the longest x1 2.4 us: shards(): chooser_deriv = jnp.dot(raw_deriv, group_square.T, precision=HIGH)]
    sub x1 -> x0, other arithmetic: 8.92 us -> none  [shards(): weights = jax.nn.softmax(present_score_entry, axis=-1)]
    unnamed x54 -> x18, local copies, waits for them, and re-layouts: 8.31 us -> 3.39 us
    reduce_sum x4 -> x2, other arithmetic: 4.48 us -> 0.23 us  [the longest x1 0.12 us: shards(): jnp.sum((joined * logit_deriv).reshape(size, heads, head), axis=(0, 2))]
    mul x0 -> x5, local copies, waits for them, and re-layouts: none -> 3.25 us  [the longest x4 3.17 us: spread_heads(): return jnp.kron(jnp.eye(heads, dtype=small.dtype), small)]
  transfers between devices with their start and end apart: 2 -> 0, of which waited for: 2 -> 0; matrix products, arithmetic and copies ran while one was open for 2% -> 0% of each run, Pallas kernels for 0% -> 0%
where the time goes in v1:
time: 101 us; the launch traced here: 99.6 us
  Pallas kernels  77.2 us (76%)
  other arithmetic  8.64 us (9%)
  local copies, waits for them, and re-layouts  8.2 us (8%)
  matrix products  4.75 us (5%)
    pallas_call x2, Pallas kernels, reduce_over(): pl.pallas_call(functools.partial(reduce_kernel, n, paired), out_shape=jax...  43.2 us
    pallas_call x1, Pallas kernels, shards(): pl.pallas_call(functools.partial(backward_kernel, heads, n_point), grid=(...  16.4 us
    pallas_call x1, Pallas kernels, shards(): pl.pallas_call(functools.partial(forward_kernel, heads), grid=(steps,), i...  11.2 us
    pallas_call x1, Pallas kernels, shards(): pl.pallas_call(functools.partial(token_kernel, heads), out_shape=[jax.Sha...  6.41 us
    unnamed x18, local copies, waits for them, and re-layouts  3.39 us
    mul x4, local copies, waits for them, and re-layouts, spread_heads(): return jnp.kron(jnp.eye(heads, dtype=small.dtype), small)  3.17 us
    dot_general x1, matrix products, shards(): chooser_deriv = jnp.dot(raw_deriv, group_square.T, precision=HIGH)  2.4 us

profile of v1, /device:TPU:29, one launch (start us, length us, event | category | flops | bytes accessed | tf_op | source)
XLA Modules:
  0.0 99.6 jit_solution(3993914970597175987)
XLA Ops:
  0.7 0.7 broadcast_divide_fusion
  1.5 0.7 convert_element_type.58
  2.2 0.7 bitcast_convert_fusion.2
  3.0 1.7 %copy.29 = bf16[256,256]{0,1:T(8,128)(2,1)} copy(bf16[256,256]{1,0:T(8,128)(2,1)} %param.10) | data formatting | bytes 262144 | tf_op args[1]
  4.6 1.5 %broadcast_multiply_fusion.2 = (f32[8,32,8,32]{3,2,1,0:T(8,128)}, f32[8,32,8,32]{3,2,1,0:T(8,128)S(1)}, f32[8,32,8,32]{3,2,1,0:T(8,128)S(1)}, f32[8,32,8,32]{3,2,1,0:T(8,128)S(1)}) fusion(f32[32,32]{1,0:T(8,128)S(1)} %get-tuple-element.62, f32[8,8]{1,0:T(8,128)S(1)} %fusion.5, f32[32,32]{1,0:T(8,128)S(1)} %get-tuple-element.64, ...), kind=kLoop, calls=%fused_computation.5 | loop fusion | flops 262144 | bytes 1065216 | tf_op jit(solution)/shard_map/jit(kron)/mul | solution.py:276
  6.1 2.2 %mul.158 = f32[1,256,256]{2,1,0:T(8,128)} reshape(f32[8,32,8,32]{3,2,1,0:T(8,128)} %get-tuple-element.65) | data formatting | bytes 524288 | tf_op jit(solution)/shard_map/jit(kron)/mul | solution.py:276
  8.7 0.3 mul.161
  9.0 0.3 mul.164
  9.6 0.9 pad_maximum_fusion.maps_ref
  10.6 1.1 %fusion = (bf16[256,256]{1,0:T(8,128)(2,1)}, bf16[256,256]{1,0:T(8,128)(2,1)}, f32[256,256]{1,0:T(8,128)S(1)}) fusion(f32[256]{0:T(256)S(1)} %mul.153, f32[256,256]{1,0:T(8,128)S(1)} %mul.152, bf16[256,256]{1,0:T(8,128)(2,1)S(1)} %copy-done), kind=kOutput, calls=%fused_computation.9 | convolution fusion | flops 201654272 | bytes 918528 | tf_op jit(solution)/shard_map/dot_general | solution.py:302
  11.7 11.2 %shard_map.160 = (bf16[256,4096]{1,0:T(8,128)(2,1)}, f32[256,4096]{1,0:T(8,128)}, bf16[256,4096]{1,0:T(8,128)(2,1)}, f32[128,256]{1,0:T(8,128)}) custom-call(bf16[4096,256]{1,0:T(8,128)(2,1)} %bitcast.41, bf16[4096,256]{1,0:T(8,128)(2,1)} %bitcast.43, bf16[256,256]{1,0:T(8,128)(2,1)} %bitcast.50, bf16[256,256]{1,0:T(8,128)(2,1)} %get-tuple-element.61.hi_ref, ...), custom_call_target="tpu_custom_call" | custom-call | tf_op jit(solution)/shard_map/pallas_call | solution.py:317
  22.8 11.9 %shard_map.161 = f32[8,16,256]{2,1,0:T(8,128)} custom-call(f32[8,16,256]{2,1,0:T(8,128)} %bitcast.54), custom_call_target="tpu_custom_call" | custom-call | tf_op jit(solution)/shard_map/pallas_call | solution.py:258
  34.8 6.4 %shard_map.162 = (bf16[256,256]{1,0:T(8,128)(2,1)}, bf16[256,256]{1,0:T(8,128)(2,1)}, f32[256,128]{1,0:T(8,128)}, f32[3,32,256]{2,1,0:T(8,128)}) custom-call(f32[128,256]{1,0:T(8,128)} %bitcast.53, f32[3,256,256]{2,1,0:T(8,128)} %pad_maximum_fusion.maps_ref), custom_call_target="tpu_custom_call" | custom-call | tf_op jit(solution)/shard_map/pallas_call | solution.py:333
  41.2 16.4 %shard_map.163 = (bf16[4096,256]{1,0:T(8,128)(2,1)}, bf16[4096,256]{1,0:T(8,128)(2,1)}, f32[896,256]{1,0:T(8,128)}) custom-call(bf16[4096,256]{1,0:T(8,128)(2,1)} %bitcast.42, bf16[4096,256]{1,0:T(8,128)(2,1)} %bitcast.44, bf16[256,4096]{1,0:T(8,128)(2,1)} %get-tuple-element.20.vt_ref, f32[256,4096]{1,0:T(8,128)} %get-tuple-element.21.wt_ref, ...), custom_call_target="tpu_custom_call" | custom-call | tf_op jit(solution)/shard_map/pallas_call | solution.py:343
  57.6 31.3 %shard_map.164 = f32[2,8,56,256]{3,2,1,0:T(8,128)} custom-call(f32[2,8,56,256]{3,2,1,0:T(8,128)} %bitcast.52), custom_call_target="tpu_custom_call" | custom-call | tf_op jit(solution)/shard_map/pallas_call | solution.py:258
  88.9 2.4 %fusion.2 = f32[256,256]{1,0:T(8,128)} fusion(f32[256,256]{1,0:T(8,128)S(1)} %mul.152, f32[896,256]{1,0:T(8,128)} %bitcast.45, f32[256]{0:T(256)S(1)} %broadcast_multiply_fusion.5), kind=kOutput, calls=%fused_computation.15 | convolution fusion | flops 201392128 | bytes 787456 | tf_op jit(solution)/shard_map/dot_general | solution.py:371
  91.3 1.3 %slice_multiply_fusion.5 = f32[1,256]{1,0:T(1,128)} fusion(f32[896,256]{1,0:T(8,128)} %bitcast.46), kind=kLoop, calls=%fused_computation.25 | loop fusion | flops 256 | bytes 2048 | tf_op jit(solution)/shard_map/mul | solution.py:386
  92.6 0.9 slice.74
  93.5 1.3 %convolution_bitcast_fusion = f32[256,256]{0,1:T(8,128)S(1)} fusion(bf16[256,256]{1,0:T(8,128)(2,1)S(1)} %copy-done, f32[896,256]{1,0:T(8,128)} %bitcast.48, f32[256]{0:T(256)S(1)} %broadcast_multiply_fusion.5), kind=kOutput, calls=%fused_computation | convolution fusion | flops 201392128 | bytes 656384 | tf_op jit(solution)/shard_map/dot_general | solution.py:372
  94.8 0.8 slice_multiply_fusion
  95.7 0.5 multiply_divide_fusion
  96.2 0.8 copy.39
  97.3 0.6 broadcast_multiply_fusion.4
  98.9 0.7 add_bitcast_fusion
  (27 shorter events, 2.2 us)
Async XLA Ops:
  0.6 9.9 %copy-start = (bf16[256,256]{1,0:T(8,128)(2,1)S(1)}, bf16[256,256]{1,0:T(8,128)(2,1)}, u32[]{:S(2)}) copy-start(bf16[256,256]{1,0:T(8,128)(2,1)} %param.11) | copy-start | bytes 393220
  8.7 1.0 copy-start.2
  57.6 38.1 %copy-start.3 = (f32[8]{0:T(128)S(1)}, f32[8]{0:T(128)}, u32[]{:S(2)}) copy-start(f32[8]{0:T(128)} %param.13) | copy-start | bytes 100
  88.9 5.8 %copy-start.1 = (f32[2,8,56,256]{3,2,1,0:T(8,128)S(1)}, f32[2,8,56,256]{3,2,1,0:T(8,128)}, u32[]{:S(2)}) copy-start(f32[2,8,56,256]{3,2,1,0:T(8,128)} %shard_map.164) | copy-start | bytes 2752516

commit v2 on v1

--- a/solution.py
+++ b/solution.py
@@ -48,12 +48,45 @@
     return jnp.where(mask, jnp.concatenate([flat] * heads, axis=0), 0.0)
 
 
+def pick(size, head, dtype):
+    row = lax.broadcasted_iota(jnp.int32, (size, head), 0)
+    col = lax.broadcasted_iota(jnp.int32, (size, head), 1)
+    return jnp.where(row % head == col, 1.0, 0.0).astype(dtype)
+
+
+def head_column(scale_row, size, head):
+    heads = size // head
+    row = lax.broadcasted_iota(jnp.int32, (size, heads), 0) // head
+    mine = row == lax.broadcasted_iota(jnp.int32, (size, heads), 1)
+    return jnp.sum(jnp.where(mine, scale_row, 0.0), axis=1, keepdims=True), mine
+
+
+def square_transposed(group, size, head):
+    e = pick(size, head, BF16)
+    return jnp.where(block_mask(size, head), nt(nt(e, group).astype(BF16), e), 0.0)
+
+
 def forward_kernel(
-    heads, x_ref, u_ref, wp_ref, hi_ref, lo_ref, wf_ref, vt_ref, wt_ref, dmt_ref, sums_ref, acc, wacc
+    heads, x_ref, u_ref, payload_ref, chooser_ref, group_ref, scale_ref, wf_ref,
+    vt_ref, wt_ref, dmt_ref, sums_ref, wp_ref, hi_ref, lo_ref, acc, wacc
 ):
     step = pl.program_id(0)
     size, rows = wt_ref.shape
     head = size // heads
+
+    @pl.when(step == 0)
+    def _():
+        row = lax.broadcasted_iota(jnp.int32, (size, size), 0)
+        col = lax.broadcasted_iota(jnp.int32, (size, size), 1)
+        same = jnp.where(row == col, 1.0, 0.0).astype(BF16)
+        wp_ref[...] = nt(same, payload_ref[...]).astype(BF16)
+        group_t = square_transposed(group_ref[...], size, head).astype(BF16)
+        column, _ = head_column(scale_ref[...], size, head)
+        joined = nt(group_t, chooser_ref[...]) / column
+        high = joined.astype(BF16)
+        hi_ref[...] = high
+        lo_ref[...] = (joined - high.astype(F32)).astype(BF16)
+
     x = x_ref[...]
     values = nt(wp_ref[...], x).astype(BF16)
     logit = nt(hi_ref[...], x) + nt(lo_ref[...], x)
@@ -98,7 +131,7 @@
 
 
 def token_kernel(heads, sums_ref, maps_ref, att_ref, dnum_ref, dws_ref, dmap_ref):
-    size = maps_ref.shape[1]
+    size = sums_ref.shape[1]
     head = size // heads
     mask = block_mask(size, head)
     numerator = unfold(sums_ref[0:head, :], mask, heads)
@@ -107,7 +140,10 @@
     weight_sum = jnp.sum(spread, axis=1, keepdims=True) * (1.0 / head)
     reciprocal = 1.0 / (weight_sum + EPS)
     tokens = numerator * reciprocal
-    maps = [maps_ref[i] for i in range(3)]
+    e = pick(size, head, BF16)
+    maps = [
+        jnp.where(mask, nt(nn(e, maps_ref[i]).astype(BF16), e), 0.0) for i in range(3)
+    ]
     q, k, v = (nn(tokens, w, HIGH) for w in maps)
     root = 1.0 / math.sqrt(head)
     scores = jnp.where(mask, nt(q, k, HIGH) * root, -jnp.inf)
@@ -272,8 +308,30 @@
     return pieces * 8 * -(-rows // (pieces * 8))
 
 
-def spread_heads(small, heads):
-    return jnp.kron(jnp.eye(heads, dtype=small.dtype), small)
+def finish_kernel(
+    heads, scaling, grads_ref, hi_ref, lo_ref, chooser_ref, group_ref, scale_ref,
+    payload_out, chooser_out, group_out, maps_out, softness_out, final_out, shift_out,
+):
+    size = grads_ref.shape[1]
+    head = size // heads
+    mask = block_mask(size, head)
+    e = pick(size, head, F32)
+    payload_out[...] = grads_ref[0:size, :].T * scaling
+    logit_deriv = grads_ref[size : 2 * size, :]
+    column, mine = head_column(scale_ref[...], size, head)
+    raw_deriv = logit_deriv * (scaling / column)
+    group_t = square_transposed(group_ref[...], size, head)
+    chooser_out[...] = tn(raw_deriv, group_t, HIGH)
+    crossed = jnp.where(mask, nn(raw_deriv, chooser_ref[...].astype(F32), HIGH), 0.0)
+    group_out[...] = tn(e, tn(crossed, e, HIGH), HIGH)
+    joined = hi_ref[...].astype(F32) + lo_ref[...].astype(F32)
+    per_row = jnp.sum(joined * logit_deriv, axis=1, keepdims=True)
+    per_head = jnp.sum(jnp.where(mine, per_row, 0.0), axis=0, keepdims=True)
+    softness_out[...] = -scaling * per_head / scale_ref[...]
+    final_out[...] = grads_ref[2 * size : 3 * size, :] * scaling
+    shift_out[...] = grads_ref[3 * size : 3 * size + 1, :] * scaling
+    tail = 3 * size + 8
+    maps_out[...] = nn(grads_ref[tail : tail + 3 * head, :], e, HIGH) * scaling
 
 
 def shards(
@@ -297,13 +355,7 @@
     n_point = lax.axis_size("point")
     sum_rows = padded(3 * head, n_point)
     grad_rows = padded(3 * size + 8 + 3 * head, 2 * n_point)
-    inverse = jnp.repeat(1.0 / softness_scale, head)
-    group_square = spread_heads(partition_group_map.astype(F32), heads)
-    joined = jnp.dot(partition_chooser_map.astype(F32), group_square, precision=HIGH) * inverse
-    joined_t = joined.T
-    rounded = lax.reduce_precision(joined_t, 8, 7)
-    hi = rounded.astype(BF16)
-    lo = (joined_t - rounded).astype(BF16)
+    scale_row = softness_scale[None, :]
     params = pltpu.CompilerParams(
         dimension_semantics=("arbitrary",), vmem_limit_bytes=VMEM_LIMIT
     )
@@ -314,22 +366,27 @@
         return pl.BlockSpec(shape, lambda i: (0,) * len(shape))
 
     square = whole(size, size)
-    vt, wt, dmt, sums = pl.pallas_call(
+    vt, wt, dmt, sums, wp, hi, lo = pl.pallas_call(
         functools.partial(forward_kernel, heads),
         grid=(steps,),
-        in_specs=[tall, tall, square, square, square, square],
-        out_specs=[wide, wide, wide, whole(sum_rows, size)],
+        in_specs=[
+            tall, tall, square, square, whole(head, head), whole(1, heads), square,
+        ],
+        out_specs=[wide, wide, wide, whole(sum_rows, size), square, square, square],
         out_shape=[
             jax.ShapeDtypeStruct((size, points), BF16),
             jax.ShapeDtypeStruct((size, points), F32),
             jax.ShapeDtypeStruct((size, points), BF16),
             jax.ShapeDtypeStruct((sum_rows, size), F32),
-        ],
+        ]
+        + [jax.ShapeDtypeStruct((size, size), BF16)] * 3,
         scratch_shapes=[pltpu.VMEM((size, 2 * size), F32), pltpu.VMEM((size, 128), F32)],
         compiler_params=params,
-    )(x, u, payload_linear_map.T, hi, lo, final_linear_map)
+    )(
+        x, u, payload_linear_map, partition_chooser_map, partition_group_map, scale_row,
+        final_linear_map,
+    )
     sums = reduce_over(sums, n_point, False)
-    maps = jnp.stack([spread_heads(centroid_qkv_maps[i].astype(F32), heads) for i in range(3)])
     att, dnum, dws, dmap = pl.pallas_call(
         functools.partial(token_kernel, heads),
         out_shape=[
@@ -339,7 +396,7 @@
             jax.ShapeDtypeStruct((3, head, size), F32),
         ],
         compiler_params=pltpu.CompilerParams(vmem_limit_bytes=VMEM_LIMIT),
-    )(sums, maps)
+    )(sums, centroid_qkv_maps)
     resp, din, grads = pl.pallas_call(
         functools.partial(backward_kernel, heads, n_point),
         grid=(steps,),
@@ -356,34 +413,37 @@
         compiler_params=params,
     )(
         x, u, vt, wt, dmt, att, dnum, dws,
-        payload_linear_map.T, hi, lo, final_linear_map, final_shift_vector[None, :],
+        wp, hi, lo, final_linear_map, final_shift_vector[None, :],
         dmap.reshape(3 * head, size),
     )
     grads = reduce_over(grads, n_point, True)
-    tail = 3 * size + 8
-    d_maps = jnp.sum(grads[tail : tail + 3 * head].reshape(3, head, heads, head), axis=2)
     scaling = 1.0 / math.sqrt(
         batch * points * lax.axis_size("point") * lax.axis_size("dp")
     )
-    payload_deriv = grads[:size].T * scaling
-    logit_deriv = grads[size : 2 * size].T
-    raw_deriv = logit_deriv * (inverse * scaling)
-    chooser_deriv = jnp.dot(raw_deriv, group_square.T, precision=HIGH)
-    crossed = jnp.dot(partition_chooser_map.astype(F32).T, raw_deriv, precision=HIGH)
-    crossed = crossed.reshape(heads, head, heads, head)
-    group_deriv = sum(crossed[h, :, h] for h in range(heads))
-    softness_deriv = -scaling * jnp.sum((joined * logit_deriv).reshape(size, heads, head), axis=(0, 2))
-    softness_deriv = softness_deriv / softness_scale
+    square_out = jax.ShapeDtypeStruct((size, size), F32)
+    payload, chooser, group, maps, softness, final, shift = pl.pallas_call(
+        functools.partial(finish_kernel, heads, scaling),
+        out_shape=[
+            square_out,
+            square_out,
+            jax.ShapeDtypeStruct((head, head), F32),
+            jax.ShapeDtypeStruct((3 * head, head), F32),
+            jax.ShapeDtypeStruct((1, heads), F32),
+            square_out,
+            jax.ShapeDtypeStruct((1, size), F32),
+        ],
+        compiler_params=pltpu.CompilerParams(vmem_limit_bytes=VMEM_LIMIT),
+    )(grads, hi, lo, partition_chooser_map, partition_group_map, scale_row)
     return (
         resp.reshape(batch, points, size),
         din.reshape(batch, points, size),
-        payload_deriv,
-        chooser_deriv,
-        group_deriv,
-        d_maps * scaling,
-        softness_deriv,
-        grads[2 * size : 3 * size] * scaling,
-        grads[3 * size] * scaling,
+        payload,
+        chooser,
+        group,
+        maps.reshape(3, head, head),
+        softness[0],
+        final,
+        shift[0],
     )
 
 

time: 101 us -> 83.4 us (0.83)
  other arithmetic: 8.64 us -> 0 us
  local copies, waits for them, and re-layouts: 8.2 us -> 0 us
  matrix products: 4.75 us -> 0 us
  Pallas kernels: 77.2 us -> 81.5 us
    dot_general x3 -> x0, matrix products: 4.75 us -> none  [the longest x1 2.4 us: shards(): chooser_deriv = jnp.dot(raw_deriv, group_square.T, precision=HIGH)]
    mul x5 -> x0, other arithmetic: 4.16 us -> none  [the longest x1 1.5 us: spread_heads(): return jnp.kron(jnp.eye(heads, dtype=small.dtype), small)]
    pallas_call x0 -> x1, Pallas kernels: none -> 3.7 us  [shards(): pl.pallas_call(functools.partial(finish_kernel, heads, scaling), out_shap...]
    unnamed x18 -> x0, local copies, waits for them, and re-layouts: 3.39 us -> none
    mul x5 -> x0, local copies, waits for them, and re-layouts: 3.25 us -> none  [the longest x4 3.17 us: spread_heads(): return jnp.kron(jnp.eye(heads, dtype=small.dtype), small)]
    convert_element_type x3 -> x0, other arithmetic: 1.44 us -> none  [the longest x1 0.73 us: shards(): centroid_qkv_maps[i].astype(F32)]
    div x2 -> x0, other arithmetic: 1.21 us -> none  [the longest x1 0.69 us: shards(): inverse = jnp.repeat(1.0 / softness_scale, head)]
    slice x2 -> x0, local copies, waits for them, and re-layouts: 1.01 us -> none  [the longest x1 0.9 us: shards(): grads[tail:tail + 3 * head].reshape(3, head, heads, head)]
where the time goes in v2:
time: 83.4 us; the launch traced here: 82.2 us
  Pallas kernels  81.5 us (98%)
    pallas_call x2, Pallas kernels, reduce_over(): pl.pallas_call(functools.partial(reduce_kernel, n, paired), out_shape=jax...  43.4 us
    pallas_call x1, Pallas kernels, shards(): pl.pallas_call(functools.partial(backward_kernel, heads, n_point), grid=(...  16.4 us
    pallas_call x1, Pallas kernels, shards(): pl.pallas_call(functools.partial(forward_kernel, heads), grid=(steps,), i...  11.8 us
    pallas_call x1, Pallas kernels, shards(): pl.pallas_call(functools.partial(token_kernel, heads), out_shape=[jax.Sha...  6.27 us
    pallas_call x1, Pallas kernels, shards(): pl.pallas_call(functools.partial(finish_kernel, heads, scaling), out_shap...  3.7 us

profile of v2, /device:TPU:29, one launch (start us, length us, event | category | flops | bytes accessed | tf_op | source)
XLA Modules:
  0.0 82.2 jit_solution(11977095260731302258)
XLA Ops:
  0.6 11.8 %shard_map.160 = (bf16[256,4096]{1,0:T(8,128)(2,1)}, f32[256,4096]{1,0:T(8,128)}, bf16[256,4096]{1,0:T(8,128)(2,1)}, f32[128,256]{1,0:T(8,128)}, bf16[256,256]{1...) custom-call(bf16[4096,256]{1,0:T(8,128)(2,1)} %bitcast.14, bf16[4096,256]{1,0:T(8,128)(2,1)} %bitcast.16, ...), custom_call_target="tpu_custom_call" | custom-call | tf_op jit(solution)/shard_map/pallas_call | solution.py:369
  12.4 11.9 %shard_map.161 = f32[8,16,256]{2,1,0:T(8,128)} custom-call(f32[8,16,256]{2,1,0:T(8,128)} %bitcast.21), custom_call_target="tpu_custom_call" | custom-call | tf_op jit(solution)/shard_map/pallas_call | solution.py:294
  24.4 6.3 %shard_map.162 = (bf16[256,256]{1,0:T(8,128)(2,1)}, bf16[256,256]{1,0:T(8,128)(2,1)}, f32[256,128]{1,0:T(8,128)}, f32[3,32,256]{2,1,0:T(8,128)}) custom-call(f32[128,256]{1,0:T(8,128)} %bitcast.20, bf16[3,32,32]{2,1,0:T(8,128)(2,1)} %maps_ref.1), custom_call_target="tpu_custom_call" | custom-call | tf_op jit(solution)/shard_map/pallas_call | solution.py:390
  30.6 16.4 %shard_map.163 = (bf16[4096,256]{1,0:T(8,128)(2,1)}, bf16[4096,256]{1,0:T(8,128)(2,1)}, f32[896,256]{1,0:T(8,128)}) custom-call(bf16[4096,256]{1,0:T(8,128)(2,1)} %bitcast.15, bf16[4096,256]{1,0:T(8,128)(2,1)} %bitcast.17, bf16[256,4096]{1,0:T(8,128)(2,1)} %get-tuple-element.30.vt_ref, f32[256,4096]{1,0:T(8,128)} %get-tuple-element.31.wt_ref, ...), custom_call_target="tpu_custom_call" | custom-call | tf_op jit(solution)/shard_map/pallas_call | solution.py:400
  47.1 31.4 %shard_map.164 = f32[2,8,56,256]{3,2,1,0:T(8,128)} custom-call(f32[2,8,56,256]{3,2,1,0:T(8,128)} %bitcast.19), custom_call_target="tpu_custom_call" | custom-call | tf_op jit(solution)/shard_map/pallas_call | solution.py:294
  78.5 3.7 %shard_map.165 = (f32[256,256]{1,0:T(8,128)}, f32[256,256]{1,0:T(8,128)}, f32[32,32]{1,0:T(8,128)}, f32[96,32]{1,0:T(8,128)}, f32[1,8]{1,0:T(1,128)}, /*index=5*/f32[256,256]{1,0:T(8,128)}, f32[1,256]{1,0:T(1,128)}) custom-call(f32[896,256]{1,0:T(8,128)} %bitcast.18, bf16[256,256]{1,0:T(8,128)(2,1)} %get-tuple-element.38.hi_ref, ...), custom_call_target="tpu_custom_call" | custom-call | tf_op jit(solution)/shard_map/pallas_call | solution.py:424

commit v3 on v2

--- a/solution.py
+++ b/solution.py
@@ -68,7 +68,7 @@
 
 def forward_kernel(
     heads, x_ref, u_ref, payload_ref, chooser_ref, group_ref, scale_ref, wf_ref,
-    vt_ref, wt_ref, dmt_ref, sums_ref, wp_ref, hi_ref, lo_ref, acc, wacc
+    vt_ref, wt_ref, dmt_ref, sums_ref, hi_ref, lo_ref, hi_t_ref, lo_t_ref, wp_ref, acc, wacc
 ):
     step = pl.program_id(0)
     size, rows = wt_ref.shape
@@ -85,7 +85,10 @@
         joined = nt(group_t, chooser_ref[...]) / column
         high = joined.astype(BF16)
         hi_ref[...] = high
-        lo_ref[...] = (joined - high.astype(F32)).astype(BF16)
+        low = joined - high.astype(F32)
+        lo_ref[...] = low.astype(BF16)
+        hi_t_ref[...] = joined.T.astype(BF16)
+        lo_t_ref[...] = low.T.astype(BF16)
 
     x = x_ref[...]
     values = nt(wp_ref[...], x).astype(BF16)
@@ -167,7 +170,7 @@
 def backward_kernel(
     heads, points,
     x_ref, u_ref, vt_ref, wt_ref, dmt_ref, att_ref, dnum_ref, dws_ref,
-    wp_ref, hi_ref, lo_ref, wf_ref, shift_ref, dmap_ref,
+    payload_ref, hi_t_ref, lo_t_ref, wf_ref, shift_ref, dmap_ref,
     resp_ref, din_ref, grads_ref,
 ):
     step = pl.program_id(0)
@@ -187,12 +190,13 @@
     d_logit = (product - weights.reshape(heads, head, rows) * mean).reshape(size, rows)
     d_high = d_logit.astype(BF16)
     d_low = (d_logit - d_high.astype(F32)).astype(BF16)
-    din_ref[...] = (
-        tn(d_values, wp_ref[...])
-        + tn(d_high, hi_ref[...])
-        + tn(d_high, lo_ref[...])
-        + tn(d_low, hi_ref[...])
-    ).astype(BF16)
+    d_input = (
+        nn(payload_ref[...], d_values)
+        + nn(hi_t_ref[...], d_high)
+        + nn(lo_t_ref[...], d_high)
+        + nn(hi_t_ref[...], d_low)
+    )
+    din_ref[...] = d_input.astype(BF16).T
     ones = jnp.ones((8, rows), BF16)
     parts = (nn(d_values, x), nn(d_high, x) + nn(d_low, x), nn(mixed, u), nn(ones, u))
     spans = ((0, size), (size, 2 * size), (2 * size, 3 * size), (3 * size, 3 * size + 8))
@@ -237,20 +241,23 @@
     if paired:
         swapped, half, swap_sem, pass_sem = more
         swaps = [
-            send(x_ref.at[1 - core, k], swapped.at[k], swap_sem, k, {"dp": 1 - core})
-            for k in range(n)
+            send(x_ref.at[1 - core, k], swapped.at[k], swap_sem, i, {"dp": 1 - core})
+            for i, k in enumerate(peers + [me])
         ]
-        for k in range(n):
-            swaps[k].wait_recv()
-            half[k] = x_ref[core, k] + swapped[k]
         source, target = half, full.at[core]
     else:
         source, target = x_ref, full
-    scatter = [
-        send(source.at[peer], recv.at[o], rs_sem, o, {"point": peer})
-        for o, peer in enumerate(peers)
-    ]
-    total = source[me]
+    scatter = []
+    for o, peer in enumerate(peers):
+        if paired:
+            swaps[o].wait_recv()
+            half[peer] = x_ref[core, peer] + swapped[peer]
+        scatter.append(send(source.at[peer], recv.at[o], rs_sem, o, {"point": peer}))
+    if paired:
+        swaps[n - 1].wait_recv()
+        total = x_ref[core, me] + swapped[me]
+    else:
+        total = source[me]
     for o, copy in enumerate(scatter):
         copy.wait_recv()
         total = total + recv[o]
@@ -366,21 +373,25 @@
         return pl.BlockSpec(shape, lambda i: (0,) * len(shape))
 
     square = whole(size, size)
-    vt, wt, dmt, sums, wp, hi, lo = pl.pallas_call(
+    vt, wt, dmt, sums, hi, lo, hi_t, lo_t = pl.pallas_call(
         functools.partial(forward_kernel, heads),
         grid=(steps,),
         in_specs=[
             tall, tall, square, square, whole(head, head), whole(1, heads), square,
         ],
-        out_specs=[wide, wide, wide, whole(sum_rows, size), square, square, square],
+        out_specs=[wide, wide, wide, whole(sum_rows, size)] + [square] * 4,
         out_shape=[
             jax.ShapeDtypeStruct((size, points), BF16),
             jax.ShapeDtypeStruct((size, points), F32),
             jax.ShapeDtypeStruct((size, points), BF16),
             jax.ShapeDtypeStruct((sum_rows, size), F32),
         ]
-        + [jax.ShapeDtypeStruct((size, size), BF16)] * 3,
-        scratch_shapes=[pltpu.VMEM((size, 2 * size), F32), pltpu.VMEM((size, 128), F32)],
+        + [jax.ShapeDtypeStruct((size, size), BF16)] * 4,
+        scratch_shapes=[
+            pltpu.VMEM((size, size), BF16),
+            pltpu.VMEM((size, 2 * size), F32),
+            pltpu.VMEM((size, 128), F32),
+        ],
         compiler_params=params,
     )(
         x, u, payload_linear_map, partition_chooser_map, partition_group_map, scale_row,
@@ -413,7 +424,7 @@
         compiler_params=params,
     )(
         x, u, vt, wt, dmt, att, dnum, dws,
-        wp, hi, lo, final_linear_map, final_shift_vector[None, :],
+        payload_linear_map, hi_t, lo_t, final_linear_map, final_shift_vector[None, :],
         dmap.reshape(3 * head, size),
     )
     grads = reduce_over(grads, n_point, True)

time: 83.4 us -> 83.7 us (level)
  Pallas kernels: 81.5 us -> 82.5 us
    pallas_call x2, Pallas kernels: 43.4 us -> 44.5 us  [reduce_over(): pl.pallas_call(functools.partial(reduce_kernel, n, paired), out_shape=jax...]
where the time goes in v3:
time: 83.7 us; the launch traced here: 83.2 us
  Pallas kernels  82.5 us (99%)
    pallas_call x2, Pallas kernels, reduce_over(): pl.pallas_call(functools.partial(reduce_kernel, n, paired), out_shape=jax...  44.5 us
    pallas_call x1, Pallas kernels, shards(): pl.pallas_call(functools.partial(backward_kernel, heads, n_point), grid=(...  16.2 us
    pallas_call x1, Pallas kernels, shards(): pl.pallas_call(functools.partial(forward_kernel, heads), grid=(steps,), i...  11.9 us
    pallas_call x1, Pallas kernels, shards(): pl.pallas_call(functools.partial(token_kernel, heads), out_shape=[jax.Sha...  6.29 us
    pallas_call x1, Pallas kernels, shards(): pl.pallas_call(functools.partial(finish_kernel, heads, scaling), out_shap...  3.7 us

profile of v3, /device:TPU:29, one launch (start us, length us, event | category | flops | bytes accessed | tf_op | source)
XLA Modules:
  0.0 83.2 jit_solution(10170825121620434454)
XLA Ops:
  0.6 11.9 %shard_map.160 = (bf16[256,4096]{1,0:T(8,128)(2,1)}, f32[256,4096]{1,0:T(8,128)}, bf16[256,4096]{1,0:T(8,128)(2,1)}, f32[128,256]{1,0:T(8,128)}, bf16[256,256]{1...) custom-call(bf16[4096,256]{1,0:T(8,128)(2,1)} %bitcast.14, ...), custom_call_target="tpu_custom_call" | custom-call | tf_op jit(solution)/shard_map/pallas_call | solution.py:376
  12.6 11.9 %shard_map.161 = f32[8,16,256]{2,1,0:T(8,128)} custom-call(f32[8,16,256]{2,1,0:T(8,128)} %bitcast.21), custom_call_target="tpu_custom_call" | custom-call | tf_op jit(solution)/shard_map/pallas_call | solution.py:301
  24.5 6.3 %shard_map.162 = (bf16[256,256]{1,0:T(8,128)(2,1)}, bf16[256,256]{1,0:T(8,128)(2,1)}, f32[256,128]{1,0:T(8,128)}, f32[3,32,256]{2,1,0:T(8,128)}) custom-call(f32[128,256]{1,0:T(8,128)} %bitcast.20, bf16[3,32,32]{2,1,0:T(8,128)(2,1)} %maps_ref.1), custom_call_target="tpu_custom_call" | custom-call | tf_op jit(solution)/shard_map/pallas_call | solution.py:401
  30.8 16.2 %shard_map.163 = (bf16[4096,256]{1,0:T(8,128)(2,1)}, bf16[4096,256]{1,0:T(8,128)(2,1)}, f32[896,256]{1,0:T(8,128)}) custom-call(bf16[4096,256]{1,0:T(8,128)(2,1)} %bitcast.15, bf16[4096,256]{1,0:T(8,128)(2,1)} %bitcast.17, bf16[256,4096]{1,0:T(8,128)(2,1)} %get-tuple-element.31.vt_ref, f32[256,4096]{1,0:T(8,128)} %get-tuple-element.32.wt_ref, ...), custom_call_target="tpu_custom_call" | custom-call | tf_op jit(solution)/shard_map/pallas_call | solution.py:411
  47.0 32.5 %shard_map.164 = f32[2,8,56,256]{3,2,1,0:T(8,128)} custom-call(f32[2,8,56,256]{3,2,1,0:T(8,128)} %bitcast.19), custom_call_target="tpu_custom_call" | custom-call | tf_op jit(solution)/shard_map/pallas_call | solution.py:301
  79.5 3.7 %shard_map.165 = (f32[256,256]{1,0:T(8,128)}, f32[256,256]{1,0:T(8,128)}, f32[32,32]{1,0:T(8,128)}, f32[96,32]{1,0:T(8,128)}, f32[1,8]{1,0:T(1,128)}, /*index=5*/f32[256,256]{1,0:T(8,128)}, f32[1,256]{1,0:T(1,128)}) custom-call(f32[896,256]{1,0:T(8,128)} %bitcast.18, bf16[256,256]{1,0:T(8,128)(2,1)} %get-tuple-element.44.hi_ref, ...), custom_call_target="tpu_custom_call" | custom-call | tf_op jit(solution)/shard_map/pallas_call | solution.py:435
